TPU v7x, 32 devices: a whole 2x2x4 slice. The times are simulated.
32 devices in a mesh: dp: 2 (over x), wide: 16 (over z, y, core).
Axes of the slice: x: 2, y: 2, z: 4, core: 2. Of those that a mesh axis runs over, the one named last changes fastest.
Arguments:
- features: bfloat16 [2, 128, 64, 2048], P('dp', 'wide'), may hold values from -28 to 28
- scale_sizes: int32 [2, 4], P('dp'), may hold values from 12 to 32, as said below
- cotangent: bfloat16 [2, 256, 8192], P('dp', 'wide'), may hold values from -6 to 6
- branch_weight: float32 [29, 256, 2048], P(None, 'wide'), may hold values from -0.088388348 to 0.088388348
- branch_first: float32 [29, 256, 2048], P(None, 'wide'), may hold values from -12 to 12
- branch_second: float32 [29, 256, 2048], P(None, 'wide'), may hold values from 0.5 to 2
- head_weight: float32 [256, 1280], P('wide'), may hold values from -0.15625 to 0.15625
- head_first: float32 [256, 1280], P('wide'), may hold values from -24 to 24
- head_second: float32 [256, 1280], P('wide'), may hold values from 2 to 8
- norm_params: float32 [2, 6, 256], P(None, None, 'wide'), may hold values from -1 to 2
- norm_first: float32 [2, 6, 256], P(None, None, 'wide'), may hold values from -24 to 24
- norm_second: float32 [2, 6, 256], P(None, None, 'wide'), may hold values from 1 to 4
- running_stats: float32 [2, 6, 256], P(None, None, 'wide'), may hold values from 0.02 to 0.2
Outputs:
- head_output: bfloat16 [2, 256, 8192], P('dp', 'wide')
- input_grad: bfloat16 [2, 128, 64, 2048], P('dp', 'wide')
- branch_grads: float32 [29, 256, 2048], P(None, 'wide')
- branch_means: float32 [29, 256, 2048], P(None, 'wide')
- branch_squares: float32 [29, 256, 2048], P(None, 'wide')
- branch_updated: float32 [29, 256, 2048], P(None, 'wide')
- head_grads: float32 [256, 1280], P('wide')
- head_means: float32 [256, 1280], P('wide')
- head_squares: float32 [256, 1280], P('wide')
- head_updated: float32 [256, 1280], P('wide')
- norm_grads: float32 [2, 6, 256], P(None, None, 'wide')
- norm_means: float32 [2, 6, 256], P(None, None, 'wide')
- norm_squares: float32 [2, 6, 256], P(None, None, 'wide')
- norm_updated: float32 [2, 6, 256], P(None, None, 'wide')
- running_next: float32 [2, 6, 256], P(None, None, 'wide')
Inputs may be any that keep to these rules, and one draw needn't show every extreme that they name: `scale_sizes`: image i of index g of dp has valid rows 0 to s - 1 and valid columns 0 to 2 s - 1 of its slot, s the entry.
All inputs are finite; a program needn't handle non-finite values.
Results may differ from a plain program's by a relative error of at most 0.02.
Values may be sent and summed in bfloat16 or wider, within the bound.
No kernel may reach another device: no remote copies, remote signals or barrier semaphores. Data moves between devices by JAX's collectives and lax.ppermute only.
A program may use at most 320 MiB of HBM per device.

v0:
```python
import jax
import jax.numpy as jnp
from jax import lax
from jax.sharding import PartitionSpec as P

STEP = 10


dilations = (6, 12, 18)
epsilon = 1e-05
momentum = 0.1
first_decay = 0.9
second_decay = 0.999
conv_rate = 0.02
norm_rate = 0.4
weight_decay = 0.0001
adam_floor = 1e-08


def tap_offsets():
    offsets = []
    for dilation in dilations:
        for row_step in range(3):
            for col_step in range(3):
                offsets.append(((row_step - 1) * dilation, (col_step - 1) * dilation))
    return offsets


def shift_slot(values_in, row_off, col_off):
    height = values_in.shape[-3]
    breadth = values_in.shape[-2]
    row_pad = abs(row_off)
    col_pad = abs(col_off)
    pad_widths = [(0, 0)] * (values_in.ndim - 3) + [(row_pad, row_pad), (col_pad, col_pad), (0, 0)]
    padded = jnp.pad(values_in, pad_widths)
    row_first = row_pad + row_off
    col_first = col_pad + col_off
    padded = lax.slice_in_dim(padded, row_first, row_first + height, axis=values_in.ndim - 3)
    return lax.slice_in_dim(padded, col_first, col_first + breadth, axis=values_in.ndim - 2)


def slot_inside(heights, slot_rows, columns):
    row_ids = jnp.arange(slot_rows, dtype=jnp.int32)[:, None]
    col_ids = jnp.arange(columns, dtype=jnp.int32)[None, :]
    extent = heights[..., None, None]
    return jnp.logical_and(row_ids < extent, col_ids < 2 * extent).astype(jnp.float32)


def gelu_back(pre_value, gradient):
    return jax.vjp(jax.nn.gelu, pre_value)[1](gradient)[0]


def adamw_update(parameter, gradient, moment_one, moment_two, step_rate, decay_rate):
    first_new = first_decay * moment_one + (1.0 - first_decay) * gradient
    second_new = second_decay * moment_two + (1.0 - second_decay) * gradient * gradient
    first_hat = first_new / (1.0 - first_decay**STEP)
    second_hat = second_new / (1.0 - second_decay**STEP)
    updated = parameter - step_rate * (
        first_hat / (jnp.sqrt(second_hat) + adam_floor) + decay_rate * parameter
    )
    return (first_new, second_new, updated)


def local(
    features,
    scale_sizes,
    cotangent,
    branch_weight,
    branch_first,
    branch_second,
    head_weight,
    head_first,
    head_second,
    norm_params,
    norm_first,
    norm_second,
    running_stats,
):
    wide_count = lax.axis_size("wide")
    group_count = lax.axis_size("dp")
    strip_rows = features.shape[1]
    columns = features.shape[2]
    channels_in = features.shape[3]
    total_rows = strip_rows * wide_count
    image_count = scale_sizes.shape[1]
    slot_rows = total_rows // image_count
    tap_count = branch_weight.shape[0]
    local_ch = branch_weight.shape[1]
    all_ch = local_ch * wide_count
    heights = scale_sizes[0]
    inside = slot_inside(heights, slot_rows, columns)
    weighted = inside[..., None]
    image_areas = (2 * heights * heights).astype(jnp.float32)
    own_start = lax.axis_index("wide") * strip_rows
    own_inside = lax.dynamic_slice_in_dim(
        inside.reshape(total_rows, columns), own_start, strip_rows, 0
    )
    masked = features * own_inside[None, :, :, None].astype(jnp.bfloat16)
    conv_weights = branch_weight.astype(jnp.bfloat16)
    conv_rows = conv_weights.reshape(tap_count * local_ch, channels_in)
    gathered = lax.all_gather(masked, "wide", axis=1, tiled=True)
    product = lax.dot_general(
        gathered.reshape(-1, channels_in),
        conv_rows,
        (((1,), (1,)), ((), ())),
        preferred_element_type=jnp.float32,
    )
    tap_values = product.reshape(
        gathered.shape[0], gathered.shape[1], columns, tap_count * local_ch
    )
    tap_values = tap_values.reshape(image_count, slot_rows, columns, tap_count, local_ch)
    offsets = tap_offsets()
    branch_pre = [tap_values[..., 0, :]]
    for dilation_id in range(3):
        accumulated = jnp.zeros_like(branch_pre[0])
        for position in range(9):
            row_off, col_off = offsets[9 * dilation_id + position]
            accumulated = accumulated + shift_slot(
                tap_values[..., 1 + 9 * dilation_id + position, :], row_off, col_off
            )
        branch_pre.append(accumulated)
    pooled = (
        jnp.sum(tap_values[..., tap_count - 1, :] * weighted, axis=(1, 2)) / image_areas[:, None]
    )
    pixel_sums = jnp.stack(
        [
            jnp.stack([jnp.sum(pre_value * weighted, axis=(0, 1, 2)) for pre_value in branch_pre]),
            jnp.stack(
                [
                    jnp.sum(pre_value * pre_value * weighted, axis=(0, 1, 2))
                    for pre_value in branch_pre
                ]
            ),
        ]
    )
    pool_sums = jnp.stack([jnp.sum(pooled, axis=0), jnp.sum(pooled * pooled, axis=0)])
    pixel_sums, pool_sums, pixel_total = lax.psum((pixel_sums, pool_sums, jnp.sum(inside)), "dp")
    image_total = float(group_count * image_count)
    gains = norm_params[0]
    shifts = norm_params[1]
    centres = pixel_sums[0] / pixel_total
    variances = pixel_sums[1] / pixel_total - centres * centres
    inverses = lax.rsqrt(variances + epsilon)
    pool_centre = pool_sums[0] / image_total
    pool_variance = pool_sums[1] / image_total - pool_centre * pool_centre
    pool_inverse = lax.rsqrt(pool_variance + epsilon)
    branch_norm = [
        gains[branch_id] * (branch_pre[branch_id] - centres[branch_id]) * inverses[branch_id]
        + shifts[branch_id]
        for branch_id in range(4)
    ]
    pool_norm = gains[4] * (pooled - pool_centre) * pool_inverse + shifts[4]
    pool_act = jnp.broadcast_to(jax.nn.gelu(pool_norm)[:, None, None, :], branch_pre[0].shape)
    concat = jnp.stack([jax.nn.gelu(normed) for normed in branch_norm] + [pool_act], axis=3).astype(
        jnp.bfloat16
    )
    full_concat = lax.all_gather(concat, "wide", axis=4, tiled=True)
    head_low = head_weight.astype(jnp.bfloat16).reshape(local_ch, 5, all_ch)
    head_pre = jnp.einsum(
        "ihwbc,obc->ihwo", full_concat, head_low, preferred_element_type=jnp.float32
    )
    head_sums = jnp.stack(
        [
            jnp.sum(head_pre * weighted, axis=(0, 1, 2)),
            jnp.sum(head_pre * head_pre * weighted, axis=(0, 1, 2)),
        ]
    )
    head_sums = lax.psum(head_sums, "dp")
    head_centre = head_sums[0] / pixel_total
    head_variance = head_sums[1] / pixel_total - head_centre * head_centre
    head_inverse = lax.rsqrt(head_variance + epsilon)
    head_norm = gains[5] * (head_pre - head_centre) * head_inverse + shifts[5]
    head_values = (
        (weighted * jax.nn.gelu(head_norm))
        .astype(jnp.bfloat16)
        .reshape(total_rows * columns, local_ch)
    )
    head_output = jnp.transpose(head_values).reshape(1, local_ch, total_rows * columns)
    grad_out = (
        jnp.transpose(cotangent[0])
        .astype(jnp.float32)
        .reshape(image_count, slot_rows, columns, local_ch)
    )
    head_delta = gelu_back(head_norm, weighted * grad_out)
    head_hat = (head_pre - head_centre) * head_inverse
    head_moments = lax.psum(
        jnp.stack(
            [jnp.sum(head_delta, axis=(0, 1, 2)), jnp.sum(head_delta * head_hat, axis=(0, 1, 2))]
        ),
        "dp",
    )
    unit_grads = (
        weighted
        * (
            gains[5]
            * head_inverse
            * (head_delta - (head_moments[0] + head_hat * head_moments[1]) / pixel_total)
        )
    ).astype(jnp.bfloat16)
    head_wgrad = jnp.einsum(
        "ihwbc,ihwo->obc", full_concat, unit_grads, preferred_element_type=jnp.float32
    )
    concat_terms = jnp.einsum(
        "ihwo,obc->ihwbc", unit_grads, head_low, preferred_element_type=jnp.float32
    )
    concat_delta = lax.psum_scatter(
        concat_terms.astype(jnp.bfloat16), "wide", scatter_dimension=4, tiled=True
    ).astype(jnp.float32)
    branch_delta = [
        gelu_back(branch_norm[branch_id], concat_delta[..., branch_id, :]) for branch_id in range(4)
    ]
    branch_hat = [
        (branch_pre[branch_id] - centres[branch_id]) * inverses[branch_id] for branch_id in range(4)
    ]
    pixel_moments = jnp.stack(
        [
            jnp.stack(
                [jnp.sum(delta_value * weighted, axis=(0, 1, 2)) for delta_value in branch_delta]
            ),
            jnp.stack(
                [
                    jnp.sum(delta_value * hat_value * weighted, axis=(0, 1, 2))
                    for delta_value, hat_value in zip(branch_delta, branch_hat)
                ]
            ),
        ]
    )
    pool_delta = gelu_back(pool_norm, jnp.sum(concat_delta[..., 4, :], axis=(1, 2)))
    pool_hat = (pooled - pool_centre) * pool_inverse
    pool_moments = jnp.stack([jnp.sum(pool_delta, axis=0), jnp.sum(pool_delta * pool_hat, axis=0)])
    pixel_moments, pool_moments = lax.psum((pixel_moments, pool_moments), "dp")
    branch_back = [
        weighted
        * (
            gains[branch_id]
            * inverses[branch_id]
            * (
                branch_delta[branch_id]
                - (
                    pixel_moments[0, branch_id]
                    + branch_hat[branch_id] * pixel_moments[1, branch_id]
                )
                / pixel_total
            )
        )
        for branch_id in range(4)
    ]
    pool_grad = (
        gains[4]
        * pool_inverse
        * (pool_delta - (pool_moments[0] + pool_hat * pool_moments[1]) / image_total)
    )
    tap_list = [branch_back[0]]
    for dilation_id in range(3):
        for position in range(9):
            row_off, col_off = offsets[9 * dilation_id + position]
            tap_list.append(shift_slot(branch_back[1 + dilation_id], -row_off, -col_off))
    tap_list.append(weighted * (pool_grad / image_areas[:, None])[:, None, None, :])
    tap_grads = jnp.stack(tap_list, axis=3).astype(jnp.bfloat16)
    grad_rows = tap_grads.reshape(total_rows, columns, tap_count * local_ch)
    conv_grad = lax.dot_general(
        grad_rows.reshape(-1, tap_count * local_ch),
        gathered.reshape(-1, channels_in),
        (((0,), (0,)), ((), ())),
        preferred_element_type=jnp.float32,
    )
    conv_grad, head_wgrad = (
        lax.psum(conv_grad.astype(jnp.bfloat16), "dp").astype(jnp.float32),
        lax.psum(head_wgrad.astype(jnp.bfloat16), "dp").astype(jnp.float32),
    )
    grad_flat = grad_rows.reshape(total_rows * columns, tap_count * local_ch)
    input_term = lax.psum_scatter(
        jnp.dot(grad_flat, conv_rows, preferred_element_type=jnp.float32).astype(jnp.bfloat16),
        "wide",
        scatter_dimension=0,
        tiled=True,
    ).astype(jnp.float32)
    input_grad = (
        input_term.reshape(1, strip_rows, columns, channels_in) * own_inside[None, :, :, None]
    ).astype(jnp.bfloat16)
    norm_grads = jnp.stack(
        [
            jnp.concatenate([pixel_moments[1], pool_moments[1][None], head_moments[1][None]]),
            jnp.concatenate([pixel_moments[0], pool_moments[0][None], head_moments[0][None]]),
        ]
    )
    branch_grads = conv_grad.reshape(tap_count, local_ch, channels_in)
    head_grads = head_wgrad.reshape(local_ch, 5 * all_ch)
    all_centres = jnp.concatenate([centres, pool_centre[None], head_centre[None]])
    all_variances = jnp.concatenate([variances, pool_variance[None], head_variance[None]])
    factors = jnp.where(
        jnp.arange(6) == 4, image_total / (image_total - 1.0), pixel_total / (pixel_total - 1.0)
    )
    running_next = (1.0 - momentum) * running_stats + momentum * jnp.stack(
        [all_centres, all_variances * factors[:, None]]
    )
    branch_means, branch_squares, branch_updated = adamw_update(
        branch_weight, branch_grads, branch_first, branch_second, conv_rate, weight_decay
    )
    head_means, head_squares, head_updated = adamw_update(
        head_weight, head_grads, head_first, head_second, conv_rate, weight_decay
    )
    norm_means, norm_squares, norm_updated = adamw_update(
        norm_params, norm_grads, norm_first, norm_second, norm_rate, 0.0
    )
    return (
        head_output,
        input_grad,
        branch_grads,
        branch_means,
        branch_squares,
        branch_updated,
        head_grads,
        head_means,
        head_squares,
        head_updated,
        norm_grads,
        norm_means,
        norm_squares,
        norm_updated,
        running_next,
    )


def solution(mesh):
    placed = (
        P("dp", "wide", None, None),
        P("dp", None),
        P("dp", "wide", None),
        P(None, "wide", None),
        P(None, "wide", None),
        P(None, "wide", None),
        P("wide", None),
        P("wide", None),
        P("wide", None),
        P(None, None, "wide"),
        P(None, None, "wide"),
        P(None, None, "wide"),
        P(None, None, "wide"),
    )
    return jax.shard_map(
        local,
        mesh=mesh,
        in_specs=placed,
        out_specs=(
            P("dp", "wide", None),
            P("dp", "wide", None, None),
            P(None, "wide", None),
            P(None, "wide", None),
            P(None, "wide", None),
            P(None, "wide", None),
            P("wide", None),
            P("wide", None),
            P("wide", None),
            P("wide", None),
            P(None, None, "wide"),
            P(None, None, "wide"),
            P(None, None, "wide"),
            P(None, None, "wide"),
            P(None, None, "wide"),
        ),
        check_vma=False,
    )
```

profile of v0, /device:TPU:0, one launch (start us, length us, event | category | flops | bytes accessed | tf_op | source)
XLA Modules:
  0.0 1575.3 jit_solution(5025465788158088734)
XLA Ops:
  18.4 165.6 %all-gather.3.cloned.1.call-done = bf16[1,128,64,2048]{3,2,0,1:T(8,128)(2,1)} async-done(((bf16[1,8,64,2048]{3,2,0,1:T(8,128)(2,1)}), bf16[1,128,64,2048]{3,2,0,1:T(8,128)(2,1)}) %all-gather.3.cloned.1.call-update) | async-done | bytes 33554448 | tf_op jit(solution)/shard_map/all_gather | solution.py:101
  184.1 40.8 %fusion.6 = f32[4,32,64,29,16]{2,3,4,1,0:T(8,128)} fusion(bf16[4,32,64,2048,1]{3,2,4,1,0:T(8,128)(2,1)} %bitcast.515, bf16[29,16,2048,1,1]{2,1,0,4,3:T(8,128)(2,1)S(1)} %convert_bitcast_fusion.1), kind=kOutput, calls=%fused_computation.21 | convolution fusion | flops 15569256448 | bytes 50659328 | tf_op jit(solution)/shard_map/dot_general | solution.py:102
  224.9 32.3 %fusion.164 = (f32[4,32,64,1,16]{2,3,4,1,0:T(1,128)S(1)}, f32[4,32,64,1,16]{2,3,4,1,0:T(1,128)S(1)}, f32[4,32,64,1,16]{2,3,4,1,0:T(1,128)S(1)}, f32[4,32,64,1,16...) fusion(f32[4,32,64,29,16]{2,3,4,1,0:T(8,128)} %fusion.6), kind=kLoop, calls=%fused_computation.351 | loop fusion | bytes 10485760 | tf_op jit(solution)/shard_map/slice | solution.py:119
  257.3 61.0 %fusion.163 = (f32[4,32,64,1,16]{2,3,4,1,0:T(1,128)}, f32[4,32,64,1,16]{2,3,4,1,0:T(1,128)}, f32[4,32,64,1,16]{2,3,4,1,0:T(1,128)}, f32[4,32,64,1,16]{2,3,4,1,0:...) fusion(f32[4,32,64,29,16]{2,3,4,1,0:T(8,128)} %fusion.6), kind=kLoop, calls=%fused_computation.350 | loop fusion | bytes 19922944 | tf_op jit(solution)/shard_map/slice | solution.py:119
  318.3 8.9 multiply_reduce_fusion.19
  329.2 5.9 all-reduce.34
  353.8 202.9 %all-gather.5.cloned.1.call-done = bf16[4,32,64,5,256]{2,1,3,0,4:T(8,128)(2,1)} async-done(((bf16[4,32,64,5,16]{2,1,3,0,4:T(8,128)(2,1)}), bf16[4,32,64,5,256]{2,1,3,0,4:T(8,128)(2,1)}) %all-gather.5.cloned.1.call-update) | async-done | bytes 20971536 | tf_op jit(solution)/shard_map/all_gather | solution.py:157
  556.8 37.9 %multiply_reduce_fusion.10 = (f32[16]{0:T(128)S(1)}, f32[16]{0:T(128)S(1)}, f32[4,32,64,16]{2,3,1,0:T(8,128)}) fusion(f32[4,32,64]{2,1,0:T(8,128)S(1)} %copy-done.2, bf16[4,32,64,5,256]{2,1,3,0,4:T(8,128)(2,1)} %all-gather.5.cloned.1.call-done, bf16[16,5,256,1,1]{2,1,0,4,3:T(8,128)(2,1)S(1)} %bitcast.482), kind=kOutput, calls=%fused_computation.152 | convolution fusion | flops 336199680 | bytes 21569664 | tf_op jit(solution)/shard_map/ihwbc,obc->ihwo/dot_general | solution.py:159
  594.7 5.3 psum.66
  601.9 4.2 fusion.148
  606.2 4.9 psum.67
  611.7 12.3 convolution_convert_fusion.1
  624.1 57.2 %copy.364 = bf16[4,32,64,5,256]{2,1,3,0,4:T(8,128)(2,1)} copy(bf16[4,32,64,5,256]{4,2,3,1,0:T(8,128)(2,1)} %convolution_convert_fusion.1) | data formatting | bytes 41943040 | tf_op jit(solution)/shard_map/convert_element_type | solution.py:207
  685.2 396.8 %reduce-scatter.3.cloned.1.call-done = bf16[4,32,64,5,16]{2,1,3,0,4:T(8,128)(2,1)} async-done(((bf16[4,32,64,5,256]{2,1,3,0,4:T(8,128)(2,1)}), bf16[4,32,64,5,16]{2,1,3,0,4:T(8,128)(2,1)}) %reduce-scatter.3.cloned.1.call-update) | async-done | bytes 1310736 | tf_op jit(solution)/shard_map/reduce_scatter | solution.py:206
  1087.8 5.8 multiply_reduce_fusion.7
  1093.7 5.2 all-reduce.33
  1112.6 11.2 copy.366
  1123.8 20.5 %convert_element_type.154 = bf16[8192,464]{0,1:T(8,128)(2,1)} reshape(bf16[4,32,64,29,16]{2,1,0,4,3:T(8,128)(2,1)} %copy.366) | data formatting | bytes 15204352 | tf_op jit(solution)/shard_map/convert_element_type | solution.py:259
  1144.3 25.0 %convolution_convert_fusion.2 = bf16[464,2048]{1,0:T(8,128)(2,1)} fusion(bf16[8192,464]{0,1:T(8,128)(2,1)} %convert_element_type.154, bf16[8192,2048]{1,0:T(8,128)(2,1)} %bitcast.516), kind=kOutput, calls=%fused_computation.12 | convolution fusion | flops 15570206720 | bytes 43057152 | tf_op jit(solution)/shard_map/dot_general | solution.py:261
  1169.4 25.4 %convolution_convert_fusion = bf16[8192,2048]{1,0:T(8,128)(2,1)} fusion(bf16[8192,464]{0,1:T(8,128)(2,1)} %convert_element_type.154, bf16[464,2048]{1,0:T(8,128)(2,1)S(1)} %bitcast.479), kind=kOutput, calls=%fused_computation.4 | convolution fusion | flops 15586033664 | bytes 43057152 | tf_op jit(solution)/shard_map/dot_general | solution.py:273
  1197.2 27.0 %fusion.17 = bf16[5,2,8,256]{3,2,1,0:T(8,128)(2,1)S(1)} fusion(bf16[4,32,64,5,256]{2,1,3,0,4:T(8,128)(2,1)} %all-gather.5.cloned.1.call-done, f32[4,32,64,16]{2,3,1,0:T(8,128)S(1)} %copy-done.9, f32[4,32,64,16]{2,3,1,0:T(8,128)S(1)} %copy-done.8, f32[]{:T(128)} %get-tuple-element.146, f32[16]{0:T(128)S(1)} %get-tuple-element.256, ...), kind=kOutput, calls=%fused_computation.55 | convolution fusion | flops 336744448 | bytes 22094148 | tf_op jit(solution)/shard_map/ihwbc,ihwo->obc/dot_general | solution.py:200
  1225.5 8.5 psum.71
  1237.4 13.9 multiply_subtract_fusion
  1251.3 313.7 %reduce-scatter.5.cloned.1.call-done = bf16[512,2048]{1,0:T(8,128)(2,1)} async-done(((bf16[8192,2048]{1,0:T(8,128)(2,1)}), bf16[512,2048]{1,0:T(8,128)(2,1)}) %reduce-scatter.5.cloned.1.call-update) | async-done | bytes 2097168 | tf_op jit(solution)/shard_map/reduce_scatter | solution.py:272
  (255 shorter events, 65.7 us)
Async XLA Ops:
  7.2 176.9 %all-gather.3.cloned.1.call-start = ((), (), s32[]{:S(2)}) async-start(), calls=%async_computation.2 | async-start | bytes 35651584 | tf_op jit(solution)/shard_map/all_gather | solution.py:101
  13.2 543.6 %all-gather.5.cloned.1.call-start = ((), (), s32[]{:S(2)}) async-start(), calls=%async_computation.3 | async-start | bytes 44564480 | tf_op jit(solution)/shard_map/all_gather | solution.py:157
  257.2 61.1 %copy-start.2 = (f32[4,32,64]{2,1,0:T(8,128)S(1)}, f32[4,32,64]{2,1,0:T(8,128)}, u32[]{:S(2)}) copy-start(f32[4,32,64]{2,1,0:T(8,128)} %and_convert_fusion) | copy-start | bytes 98308
  257.2 61.1 %copy-start.3 = (f32[4,32,64,1,16]{2,3,4,1,0:T(1,128)S(1)}, f32[4,32,64,1,16]{2,3,4,1,0:T(1,128)}, u32[]{:S(2)}) copy-start(f32[4,32,64,1,16]{2,3,4,1,0:T(1,128)} %get-tuple-element.197) | copy-start | bytes 1572868
  349.0 732.9 %reduce-scatter.3.cloned.1.call-start = ((), (), s32[]{:S(2)}) async-start(), calls=%async_computation.4 | async-start | bytes 44564480 | tf_op jit(solution)/shard_map/reduce_scatter | solution.py:206
  681.3 406.3 %copy-start.27 = (f32[16]{0:T(128)S(1)}, f32[16]{0:T(128)}, u32[]{:S(2)}) copy-start(f32[16]{0:T(128)} %get-tuple-element.224) | copy-start | bytes 196
  681.4 406.3 %copy-start.28 = (f32[16]{0:T(128)S(1)}, f32[16]{0:T(128)}, u32[]{:S(2)}) copy-start(f32[16]{0:T(128)} %get-tuple-element.225) | copy-start | bytes 196
  681.4 406.3 %copy-start.30 = (f32[16]{0:T(128)S(1)}, f32[16]{0:T(128)}, u32[]{:S(2)}) copy-start(f32[16]{0:T(128)} %copy-done.29) | copy-start | bytes 196
  681.4 406.3 %copy-start.32 = (f32[16]{0:T(128)S(1)}, f32[16]{0:T(128)}, u32[]{:S(2)}) copy-start(f32[16]{0:T(128)} %copy-done.31) | copy-start | bytes 196
  681.4 406.3 %copy-start.34 = (f32[16]{0:T(128)S(1)}, f32[16]{0:T(128)}, u32[]{:S(2)}) copy-start(f32[16]{0:T(128)} %copy-done.33) | copy-start | bytes 196
  681.4 406.3 %copy-start.36 = (f32[16]{0:T(128)S(1)}, f32[16]{0:T(128)}, u32[]{:S(2)}) copy-start(f32[16]{0:T(128)} %copy-done.35) | copy-start | bytes 196
  681.4 406.3 %copy-start.38 = (f32[16]{0:T(128)S(1)}, f32[16]{0:T(128)}, u32[]{:S(2)}) copy-start(f32[16]{0:T(128)} %copy-done.37) | copy-start | bytes 196
  681.4 406.3 %copy-start.40 = (f32[16]{0:T(128)S(1)}, f32[16]{0:T(128)}, u32[]{:S(2)}) copy-start(f32[16]{0:T(128)} %copy-done.39) | copy-start | bytes 196
  681.4 406.3 %copy-start.42 = (f32[16]{0:T(128)S(1)}, f32[16]{0:T(128)}, u32[]{:S(2)}) copy-start(f32[16]{0:T(128)} %copy-done.41) | copy-start | bytes 196
  681.4 406.3 %copy-start.44 = (f32[16]{0:T(128)S(1)}, f32[16]{0:T(128)}, u32[]{:S(2)}) copy-start(f32[16]{0:T(128)} %copy-done.43) | copy-start | bytes 196
  681.4 406.3 %copy-start.48 = (f32[16]{0:T(128)S(1)}, f32[16]{0:T(128)}, u32[]{:S(2)}) copy-start(f32[16]{0:T(128)} %get-tuple-element.218) | copy-start | bytes 196
  681.5 406.3 %copy-start.49 = (f32[16]{0:T(128)S(1)}, f32[16]{0:T(128)}, u32[]{:S(2)}) copy-start(f32[16]{0:T(128)} %get-tuple-element.219) | copy-start | bytes 196
  681.5 406.3 %copy-start.50 = (f32[16]{0:T(128)S(1)}, f32[16]{0:T(128)}, u32[]{:S(2)}) copy-start(f32[16]{0:T(128)} %get-tuple-element.220) | copy-start | bytes 196
  681.5 406.3 %copy-start.51 = (f32[16]{0:T(128)S(1)}, f32[16]{0:T(128)}, u32[]{:S(2)}) copy-start(f32[16]{0:T(128)} %get-tuple-element.221) | copy-start | bytes 196
  681.5 406.3 %copy-start.52 = (f32[16]{0:T(128)S(1)}, f32[16]{0:T(128)}, u32[]{:S(2)}) copy-start(f32[16]{0:T(128)} %get-tuple-element.222) | copy-start | bytes 196
  681.5 406.3 %copy-start.53 = (f32[16]{0:T(128)S(1)}, f32[16]{0:T(128)}, u32[]{:S(2)}) copy-start(f32[16]{0:T(128)} %get-tuple-element.223) | copy-start | bytes 196
  681.5 555.9 %all-reduce.37.cloned.1.call-start = ((), (), s32[]{:S(2)}) async-start(), calls=%async_computation.6 | async-start | bytes 3801088 | tf_op jit(solution)/shard_map/psum | solution.py:268
  1169.3 395.6 %reduce-scatter.5.cloned.1.call-start = ((), (), s32[]{:S(2)}) async-start(), calls=%async_computation.5 | async-start | bytes 35651584 | tf_op jit(solution)/shard_map/reduce_scatter | solution.py:272
  1237.4 327.6 %copy-start.23 = (f32[8,64]{1,0:T(8,128)S(1)}, f32[8,64]{1,0:T(8,128)}, u32[]{:S(2)}) copy-start(f32[8,64]{1,0:T(8,128)} %get-tuple-element.207) | copy-start | bytes 6148
  (50 other events, 863.9 us)
Sparse Core Ops, SparseCore 0:
  13.3 170.7 all-gather.2
  349.1 207.5 all-gather.4
  681.5 400.4 reduce-scatter.2
  1169.5 57.7 all-reduce.36
  1232.0 332.9 reduce-scatter.4
where the time goes:
time: 1590 us; the launch traced here: 1580 us
  waiting for transfers between devices  1080 us (68%)
  local copies, waits for them, and re-layouts  203 us (13%)
  matrix products  168 us (11%)
  other arithmetic  77.4 us (5%)
  blocking collectives  29.9 us (2%)
  between operations  17.1 us (1%)
    reduce_scatter x1, waiting for transfers between devices, local(): lax.psum_scatter(concat_terms.astype(jnp.bfloat16), 'wide', scatter_dimen...  397 us
    reduce_scatter x1, waiting for transfers between devices, local(): lax.psum_scatter(jnp.dot(grad_flat, conv_rows, preferred_element_type=jnp...  314 us
    all_gather x1, waiting for transfers between devices, local(): full_concat = lax.all_gather(concat, 'wide', axis=4, tiled=True)  203 us
    all_gather x1, waiting for transfers between devices, local(): gathered = lax.all_gather(masked, 'wide', axis=1, tiled=True)  166 us
    slice x2, local copies, waits for them, and re-layouts, local(): tap_values[..., 1 + 9 * dilation_id + position, :]  93.3 us
    convert_element_type x1, local copies, waits for them, and re-layouts, local(): concat_terms.astype(jnp.bfloat16)  57.2 us
    dot_general x1, matrix products, local(): lax.dot_general(gathered.reshape(-1, channels_in), conv_rows, (((1,), (1,...  40.8 us
    dot_general x1, matrix products, local(): jnp.einsum('ihwbc,obc->ihwo', full_concat, head_low, preferred_element_ty...  37.9 us
  transfers between devices with their start and end apart: 5, of which 4 were waited for; matrix products, arithmetic and copies ran while one was open for 5% of the time, Pallas kernels for 0%

commit v1 on v0

v1 whole, which is shorter than its diff:
```python
import functools

import jax
import jax.numpy as jnp
from jax import lax
from jax.experimental import pallas as pl
from jax.experimental.pallas import tpu as pltpu
from jax.sharding import Mesh, PartitionSpec as P

STEP = 10


dilations = (6, 12, 18)
epsilon = 1e-05
momentum = 0.1
first_decay = 0.9
second_decay = 0.999
conv_rate = 0.02
norm_rate = 0.4
weight_decay = 0.0001
adam_floor = 1e-08

LANES = 128
VMEM_LIMIT = 56 * 1024 * 1024
PLANE = ("z", "y", "c")
QUAD = ("y", "c")
SWAP = [(0, 1), (1, 0)]
PAIR = [(0, 1), (1, 0), (2, 3), (3, 2)]
MID = [(1, 2), (2, 1)]
OUTWARD = [(1, 0), (2, 3)]
INWARD = [(0, 1), (3, 2)]

bf16 = jnp.bfloat16
f32 = jnp.float32
barrier = lax.optimization_barrier


def gelu_back(pre_value, gradient):
    return jax.vjp(jax.nn.gelu, pre_value)[1](gradient)[0]


def adamw_update(parameter, gradient, moment_one, moment_two, step_rate, decay_rate):
    first_new = first_decay * moment_one + (1.0 - first_decay) * gradient
    second_new = second_decay * moment_two + (1.0 - second_decay) * gradient * gradient
    first_hat = first_new / (1.0 - first_decay**STEP)
    second_hat = second_new / (1.0 - second_decay**STEP)
    updated = parameter - step_rate * (
        first_hat / (jnp.sqrt(second_hat) + adam_floor) + decay_rate * parameter
    )
    return (first_new, second_new, updated)


def total_over(value, axes):
    count = 1
    for axis in axes:
        count *= lax.axis_size(axis)
    spread = jnp.broadcast_to(value[None], (count,) + value.shape)
    return jnp.sum(lax.all_to_all(spread, axes, 0, 0, tiled=True), axis=0)


def lane_masks(columns):
    lane = lax.broadcasted_iota(jnp.int32, (1, LANES), 1) % columns
    masks = {}
    for dilation in dilations:
        for off in (-dilation, dilation):
            moved = lane + off
            masks[off] = jnp.logical_and(moved >= 0, moved < columns)
    return masks


def forward_kernel(columns, split, sel_ref, x_ref, wz_ref, wx_ref, mask_ref, pre_ref, stat_ref, taps):
    step = pl.program_id(0)
    half = wz_ref.shape[0]
    block = x_ref.shape[0]
    sel = sel_ref[0]
    contract = (((1,), (1,)), ((), ()))
    pixels = x_ref[...]
    cols = pl.ds(pl.multiple_of(step * block, block), block)
    taps[pl.ds(pl.multiple_of(sel * half, 16), half), cols] = lax.dot_general(
        wz_ref[...], pixels, contract, preferred_element_type=f32
    )
    taps[pl.ds(pl.multiple_of((1 - sel) * half, 16), half), cols] = lax.dot_general(
        wx_ref[...], pixels, contract, preferred_element_type=f32
    )

    @pl.when(step == pl.num_programs(0) - 1)
    def _():
        total = taps.shape[1]
        tiles = total // LANES
        chans = pre_ref.shape[1]
        masks = lane_masks(columns)

        def rows_of(tap):
            first = tap * chans if tap <= split else (tap + 1) * chans
            return slice(first, first + chans)

        def tile(tap, at):
            return taps[rows_of(tap), at * LANES : (at + 1) * LANES]

        sums = [jnp.zeros((chans, LANES), f32) for _ in range(4)]
        squares = [jnp.zeros((chans, LANES), f32) for _ in range(4)]
        pooled = jnp.zeros((chans, LANES), f32)
        for at in range(tiles):
            lanes = slice(at * LANES, (at + 1) * LANES)
            weight = mask_ref[0:1, lanes]
            for branch in range(4):
                if branch == 0:
                    value = tile(0, at)
                else:
                    dilation = dilations[branch - 1]
                    jump = dilation * columns // LANES
                    value = None
                    for b in range(3):
                        part = None
                        for a in range(3):
                            source = at + (a - 1) * jump
                            if 0 <= source < tiles:
                                term = tile(1 + 9 * (branch - 1) + 3 * a + b, source)
                                part = term if part is None else part + term
                        off = (b - 1) * dilation
                        if off != 0:
                            part = pltpu.roll(part, (-off) % LANES, 1)
                            part = jnp.where(masks[off], part, 0.0)
                        value = part if value is None else value + part
                pre_ref[branch, :, lanes] = value
                weighted = value * weight
                sums[branch] = sums[branch] + weighted
                squares[branch] = squares[branch] + weighted * value
            pooled = pooled + tile(28, at)
        lane = lax.broadcasted_iota(jnp.int32, (chans, LANES), 1)
        for branch in range(4):
            one = jnp.sum(sums[branch], axis=1, keepdims=True)
            two = jnp.sum(squares[branch], axis=1, keepdims=True)
            row = jnp.where(lane == 0, one, jnp.where(lane == 1, two, 0.0))
            if branch == 0:
                row = jnp.where(lane == 2, jnp.sum(pooled, axis=1, keepdims=True), row)
            stat_ref[branch * chans : (branch + 1) * chans, :] = row


def forward_taps(pixels, mask_row, sel, wz, wx, columns, chans, split):
    total, depth = pixels.shape
    block = total // 4
    half = wz.shape[0]
    return pl.pallas_call(
        functools.partial(forward_kernel, columns, split),
        out_shape=(
            jax.ShapeDtypeStruct((4, chans, total), f32),
            jax.ShapeDtypeStruct((4 * chans, LANES), f32),
        ),
        grid_spec=pltpu.PrefetchScalarGridSpec(
            num_scalar_prefetch=1,
            grid=(4,),
            in_specs=[
                pl.BlockSpec((block, depth), lambda i, s: (i, 0)),
                pl.BlockSpec((half, depth), lambda i, s: (0, 0)),
                pl.BlockSpec((half, depth), lambda i, s: (0, 0)),
                pl.BlockSpec((8, total), lambda i, s: (0, 0)),
            ],
            out_specs=(
                pl.BlockSpec((4, chans, total), lambda i, s: (0, 0, 0)),
                pl.BlockSpec((4 * chans, LANES), lambda i, s: (0, 0)),
            ),
            scratch_shapes=[pltpu.VMEM((2 * half, total), f32)],
        ),
        compiler_params=pltpu.CompilerParams(vmem_limit_bytes=VMEM_LIMIT),
        cost_estimate=pl.CostEstimate(
            flops=4 * half * total * depth,
            bytes_accessed=2 * total * depth + 4 * half * depth + 16 * chans * total,
            transcendentals=0,
        ),
        name="atrous_forward",
    )(sel, pixels, wz, wx, mask_row)


def weight_kernel(columns, sel_ref, g_ref, x_ref, keep_ref, send_ref, taps_ref, total_ref):
    chans = g_ref.shape[0] // 5
    half = keep_ref.shape[0]
    start = half - chans

    @pl.when(pl.program_id(0) == 0)
    def _():
        tiles = g_ref.shape[1] // LANES
        masks = lane_masks(columns)
        for at in range(tiles):
            lanes = slice(at * LANES, (at + 1) * LANES)
            taps_ref[0:chans, lanes] = g_ref[0:chans, lanes]
            taps_ref[28 * chans : 29 * chans, lanes] = g_ref[4 * chans : 5 * chans, lanes]
            for j, dilation in enumerate(dilations):
                jump = dilation * columns // LANES
                grad = g_ref[(1 + j) * chans : (2 + j) * chans, lanes].astype(f32)
                for b in range(3):
                    off = (b - 1) * dilation
                    moved = grad
                    if off != 0:
                        moved = pltpu.roll(grad, off % LANES, 1)
                        moved = jnp.where(masks[-off], moved, 0.0)
                    moved = moved.astype(bf16)
                    for a in range(3):
                        tap = 1 + 9 * j + 3 * a + b
                        rows = slice(tap * chans, (tap + 1) * chans)
                        target = at + (a - 1) * jump
                        if 0 <= target < tiles:
                            taps_ref[rows, target * LANES : (target + 1) * LANES] = moved
                        source = at - (a - 1) * jump
                        if not 0 <= source < tiles:
                            taps_ref[rows, lanes] = jnp.zeros((chans, LANES), bf16)

    total_ref[...] = jnp.dot(taps_ref[...], x_ref[...], preferred_element_type=f32)
    sel = sel_ref[0]
    keep_ref[...] = total_ref[pl.ds(pl.multiple_of(sel * start, 16), half), :].astype(bf16)
    send_ref[...] = total_ref[pl.ds(pl.multiple_of((1 - sel) * start, 16), half), :].astype(bf16)


def weight_grads(grads, pixels, sel, columns, half):
    rows, total = grads.shape
    chans = rows // 5
    depth = pixels.shape[1]
    block = depth // 4
    return pl.pallas_call(
        functools.partial(weight_kernel, columns),
        out_shape=(
            jax.ShapeDtypeStruct((half, depth), bf16),
            jax.ShapeDtypeStruct((half, depth), bf16),
            jax.ShapeDtypeStruct((29 * chans, total), bf16),
        ),
        grid_spec=pltpu.PrefetchScalarGridSpec(
            num_scalar_prefetch=1,
            grid=(4,),
            in_specs=[
                pl.BlockSpec((rows, total), lambda i, s: (0, 0)),
                pl.BlockSpec((total, block), lambda i, s: (0, i)),
            ],
            out_specs=(
                pl.BlockSpec((half, block), lambda i, s: (0, i)),
                pl.BlockSpec((half, block), lambda i, s: (0, i)),
                pl.BlockSpec((29 * chans, total), lambda i, s: (0, 0)),
            ),
            scratch_shapes=[pltpu.VMEM((29 * chans, block), f32)],
        ),
        compiler_params=pltpu.CompilerParams(vmem_limit_bytes=VMEM_LIMIT),
        cost_estimate=pl.CostEstimate(
            flops=2 * 29 * chans * total * depth,
            bytes_accessed=2 * total * depth + 8 * half * depth,
            transcendentals=0,
        ),
        name="atrous_weight_grad",
    )(sel, grads, pixels)


def input_kernel(start, sel_ref, strip_ref, *refs):
    taps = refs[0:4]
    weights = refs[4:12]
    out_ref, total = refs[12], refs[13]
    half = weights[0].shape[0]
    contract = (((0,), (0,)), ((), ()))
    for slot in range(4):
        sel = sel_ref[slot]
        for which in range(2):
            first = sel * start if which == 0 else (1 - sel) * start
            part = lax.dot_general(
                taps[slot][pl.ds(pl.multiple_of(first, 16), half), :],
                weights[2 * slot + which][...],
                contract,
                preferred_element_type=f32,
            )
            if slot == 0 and which == 0:
                total[...] = part
            else:
                total[...] += part
    out_ref[0] = total[...].astype(bf16)


def input_grads(taps, weights, sels, strips, block):
    rows, total = taps[0].shape
    half, depth = weights[0].shape
    count = strips.shape[0]
    start = rows - half
    return pl.pallas_call(
        functools.partial(input_kernel, start),
        out_shape=jax.ShapeDtypeStruct((count, block, depth), bf16),
        grid_spec=pltpu.PrefetchScalarGridSpec(
            num_scalar_prefetch=2,
            grid=(count,),
            in_specs=[pl.BlockSpec((rows, block), lambda i, s, t: (0, t[i]))] * 4
            + [pl.BlockSpec((half, depth), lambda i, s, t: (0, 0))] * 8,
            out_specs=pl.BlockSpec((1, block, depth), lambda i, s, t: (i, 0, 0)),
            scratch_shapes=[pltpu.VMEM((block, depth), f32)],
        ),
        compiler_params=pltpu.CompilerParams(vmem_limit_bytes=VMEM_LIMIT),
        cost_estimate=pl.CostEstimate(
            flops=2 * 4 * rows * block * count * depth,
            bytes_accessed=16 * half * depth + 2 * count * block * depth,
            transcendentals=0,
        ),
        name="atrous_input_grad",
    )(sels, strips, *taps, *weights)


def local(
    features,
    scale_sizes,
    cotangent,
    branch_weight,
    branch_first,
    branch_second,
    head_weight,
    head_first,
    head_second,
    norm_params,
    norm_first,
    norm_second,
    running_stats,
):
    groups = lax.axis_size("dp")
    halves = groups == 2
    images = scale_sizes.shape[1]
    x_id, z_id = lax.axis_index("dp"), lax.axis_index("z")
    quad_id = lax.axis_index("y") * 2 + lax.axis_index("c")
    wide_id = z_id * 4 + quad_id
    strip_rows, columns, depth = features.shape[1:]
    strip = strip_rows * columns
    total = 4 * strip
    tap_count, chans = branch_weight.shape[:2]
    all_ch = chans * lax.axis_size("z") * 4
    split = (tap_count - 1) // 2
    half = (split + 1) * chans
    ends = jnp.logical_or(z_id == 0, z_id == 3)
    mid = jnp.logical_not(ends)

    height = lax.dynamic_index_in_dim(scale_sizes[0], z_id, 0, keepdims=False)
    pixel = jnp.arange(total, dtype=jnp.int32)
    inside = jnp.logical_and(pixel // columns < height, pixel % columns < 2 * height).astype(f32)
    own_inside = lax.dynamic_slice_in_dim(inside, quad_id * strip, strip, 0)
    area = (2 * height * height).astype(f32)
    mask_rows = jnp.broadcast_to(inside[None], (8, total))

    low_half = branch_weight[: split + 1]
    high_half = jnp.concatenate(
        [jnp.zeros_like(branch_weight[:1]), branch_weight[split + 1 :]], axis=0
    )
    own_w = [
        part.astype(bf16).reshape(half, depth) for part in (low_half, high_half)
    ]

    masked = features[0].reshape(strip, depth) * own_inside[:, None].astype(bf16)
    over_c = lax.ppermute(masked, "c", SWAP)
    over_y = lax.ppermute(masked, "y", SWAP)
    over_yc = lax.ppermute(over_y, "c", SWAP)

    def z_chain(block):
        near = lax.ppermute(block, "z", PAIR)
        mid_one = lax.ppermute(block, "z", MID)
        mid_two = lax.ppermute(near, "z", MID)
        out_one = lax.ppermute(mid_one, "z", OUTWARD)
        out_two = lax.ppermute(mid_two, "z", OUTWARD)
        second = jnp.where(mid, mid_one, out_one)
        out_two, second = barrier((out_two, second))
        third = jnp.where(mid, mid_two, out_two)
        return near, second, third

    if halves:
        mine = jnp.where(x_id == 0, own_w[0], own_w[1])
        slots = [(mine_z, lax.ppermute(mine_z, "dp", SWAP)) for mine_z in z_chain(mine)]
        sel = x_id.astype(jnp.int32)
    else:
        lows, highs = z_chain(own_w[0]), z_chain(own_w[1])
        slots = list(zip(lows, highs))
        sel = jnp.zeros((), jnp.int32)
    zero = jnp.zeros((), jnp.int32)
    slots = [tuple(own_w)] + slots
    sels = [zero, sel, sel, sel]
    order = jnp.stack(
        [
            z_id,
            jnp.array([1, 0, 3, 2], jnp.int32)[z_id],
            jnp.array([2, 2, 1, 1], jnp.int32)[z_id],
            jnp.array([3, 3, 0, 0], jnp.int32)[z_id],
        ]
    )
    place = (order[None, :] == jnp.arange(4, dtype=jnp.int32)[:, None]).astype(f32)

    def to_canon(by_slot):
        grown = place.reshape((4, 4) + (1,) * (by_slot.ndim - 1))
        return jnp.sum(grown * by_slot[None], axis=1)

    def to_slots(by_z):
        grown = place.reshape((4, 4) + (1,) * (by_z.ndim - 1))
        return jnp.sum(grown * by_z[:, None], axis=0)

    all_norm = lax.all_gather(norm_params, PLANE, axis=0).reshape(4, 4, 2, 6, chans)
    own_norm = lax.dynamic_index_in_dim(all_norm, quad_id, 1, keepdims=False)
    slot_norm = to_slots(own_norm)
    head_norm_params = jnp.transpose(all_norm[:, :, :, 5], (2, 0, 1, 3)).reshape(2, all_ch)
    gains, shifts = slot_norm[:, 0], slot_norm[:, 1]
    projection = lax.all_gather(head_weight.astype(bf16), PLANE, axis=0, tiled=True)
    projection = projection.reshape(all_ch, 5, 4, 4, chans)
    projection = jnp.stack(
        [lax.dynamic_index_in_dim(projection, order[slot], 2, keepdims=False) for slot in range(4)],
        axis=0,
    )
    projection = jnp.transpose(projection, (1, 3, 0, 2, 4))
    pixel_proj = projection[:, :, :, :4].reshape(all_ch, 4, 16 * chans)
    pixel_proj = jnp.pad(pixel_proj, ((0, 0), (0, 0), (0, 16))).reshape(all_ch, 4 * (16 * chans + 16))
    pool_proj = projection[:, :, :, 4].astype(f32).reshape(all_ch, 16 * chans)

    cot = lax.all_to_all(cotangent[0], PLANE, 1, 0, tiled=True)

    pixels = jnp.zeros((total, depth), bf16)
    for flip, part in enumerate((masked, over_c, over_y, over_yc)):
        pixels = lax.dynamic_update_slice_in_dim(
            pixels, part, jnp.bitwise_xor(quad_id, flip) * strip, 0
        )

    pre, stats = [], []
    for slot in range(4):
        pre_part, stat_part = forward_taps(
            pixels, mask_rows, sels[slot][None], *slots[slot], columns, chans, split
        )
        pre.append(pre_part)
        stats.append(stat_part)
    stats = jnp.stack(stats).reshape(4, 4, chans, LANES)
    pooled = stats[:, 0, :, 2] / area
    image_total = float(groups * images)
    partial = jnp.concatenate(
        [
            stats[..., 0],
            stats[..., 1],
            pooled[:, None],
            (pooled * pooled)[:, None],
            jnp.broadcast_to(area, (4, 1, chans)),
        ],
        axis=1,
    )
    sums = total_over(to_canon(partial), ("dp", "z"))
    pixel_total = sums[0, 10, 0]
    counts = jnp.concatenate([jnp.full((4,), 1.0, f32) * pixel_total, jnp.full((1,), image_total, f32)])
    firsts = jnp.concatenate([sums[:, 0:4], sums[:, 8:9]], axis=1)
    seconds = jnp.concatenate([sums[:, 4:8], sums[:, 9:10]], axis=1)
    centres = firsts / counts[None, :, None]
    variances = seconds / counts[None, :, None] - centres * centres
    inverses = lax.rsqrt(variances + epsilon)
    slot_centre, slot_inverse = to_slots(centres), to_slots(inverses)

    def branch_hat(slot):
        return (pre[slot] - slot_centre[slot, :4, :, None]) * slot_inverse[slot, :4, :, None]

    def branch_norm(slot):
        return (
            gains[slot, :4, :, None] * (pre[slot] - slot_centre[slot, :4, :, None])
        ) * slot_inverse[slot, :4, :, None] + shifts[slot, :4, :, None]

    pool_norm = gains[:, 4] * (pooled - slot_centre[:, 4]) * slot_inverse[:, 4] + shifts[:, 4]
    pool_hat = (pooled - slot_centre[:, 4]) * slot_inverse[:, 4]
    pool_act = jax.nn.gelu(pool_norm).astype(bf16)

    parts = [jax.nn.gelu(branch_norm(slot)).astype(bf16) for slot in range(4)]
    concat = jnp.stack(parts).reshape(4 * 4 * chans, 4, strip)
    concat = jnp.transpose(concat, (1, 0, 2))
    extra = jnp.pad(pool_act.reshape(1, 4 * chans), ((0, 15), (0, strip - 4 * chans)))
    concat = jnp.concatenate([concat, jnp.broadcast_to(extra[None], (4, 16, strip))], axis=1)
    concat = lax.all_to_all(concat, QUAD, 0, 0, tiled=True)
    all_pool = concat[:, 16 * chans, : 4 * chans].astype(f32).reshape(16 * chans)
    concat = concat.reshape(4 * (16 * chans + 16), strip)

    unit = jnp.dot(pixel_proj, concat, preferred_element_type=f32)
    unit = unit + jnp.sum(pool_proj * all_pool[None], axis=1)[:, None]
    weighted = own_inside[None]
    head_sums = total_over(
        jnp.stack([jnp.sum(unit * weighted, axis=1), jnp.sum(unit * unit * weighted, axis=1)]),
        ("dp",) + PLANE,
    )
    head_centre = head_sums[0] / pixel_total
    head_variance = head_sums[1] / pixel_total - head_centre * head_centre
    head_inverse = lax.rsqrt(head_variance + epsilon)
    head_gain, head_shift = head_norm_params[0], head_norm_params[1]
    head_hat = (unit - head_centre[:, None]) * head_inverse[:, None]
    head_norm = (head_gain[:, None] * (unit - head_centre[:, None])) * head_inverse[
        :, None
    ] + head_shift[:, None]
    head_values = (weighted * jax.nn.gelu(head_norm)).astype(bf16)
    head_output = lax.all_to_all(head_values, PLANE, 0, 1, tiled=True)[None]
    head_delta = gelu_back(head_norm, weighted * cot.astype(f32))
    head_moments = total_over(
        jnp.stack([jnp.sum(head_delta, axis=1), jnp.sum(head_delta * head_hat, axis=1)]),
        ("dp",) + PLANE,
    )
    unit_back = (
        weighted
        * (
            (head_gain * head_inverse)[:, None]
            * (
                head_delta
                - (head_moments[0][:, None] + head_hat * head_moments[1][:, None]) / pixel_total
            )
        )
    ).astype(bf16)
    row_sums = jnp.sum(unit_back.astype(f32), axis=1)

    concat_terms = lax.dot_general(
        pixel_proj, unit_back, (((0,), (0,)), ((), ())), preferred_element_type=f32
    ).astype(bf16)
    concat_terms = concat_terms.reshape(4, 16 * chans + 16, strip)[:, : 16 * chans]
    pool_terms = jnp.sum(pool_proj * row_sums[:, None], axis=0).reshape(4, 1, 4 * chans)
    pool_high = pool_terms.astype(bf16)
    pool_low = (pool_terms - pool_high.astype(f32)).astype(bf16)
    pool_rows = jnp.pad(
        jnp.concatenate([pool_high, pool_low], axis=1),
        ((0, 0), (0, 14), (0, strip - 4 * chans)),
    )
    concat_back = lax.all_to_all(
        jnp.concatenate([concat_terms, pool_rows], axis=1), QUAD, 0, 0, tiled=True
    )
    pool_back = jnp.sum(
        concat_back[:, 16 * chans : 16 * chans + 2, : 4 * chans].astype(f32), axis=(0, 1)
    ).reshape(4, chans)
    concat_back = jnp.transpose(concat_back[:, : 16 * chans], (1, 0, 2)).reshape(
        4, 4, chans, total
    )

    def branch_delta(slot):
        return gelu_back(branch_norm(slot), concat_back[slot].astype(f32))

    pool_delta = gelu_back(pool_norm, pool_back)
    moments = []
    for slot in range(4):
        delta = branch_delta(slot) * inside
        moments.append(
            jnp.stack([jnp.sum(delta, axis=2), jnp.sum(delta * branch_hat(slot), axis=2)])
        )
    moments = jnp.concatenate(
        [jnp.stack(moments), jnp.stack([pool_delta, pool_delta * pool_hat], axis=1)[:, :, None]],
        axis=2,
    )
    moments = total_over(to_canon(moments), ("dp", "z"))
    slot_moments = to_slots(moments)
    pool_grad = (
        gains[:, 4]
        * slot_inverse[:, 4]
        * (pool_delta - (slot_moments[:, 0, 4] + pool_hat * slot_moments[:, 1, 4]) / image_total)
    ) / area

    def branch_grad(slot):
        grad = inside * (
            (gains[slot, :4] * slot_inverse[slot, :4])[..., None]
            * (
                branch_delta(slot)
                - (
                    slot_moments[slot, 0, :4, :, None]
                    + branch_hat(slot) * slot_moments[slot, 1, :4, :, None]
                )
                / pixel_total
            )
        )
        spread = inside * pool_grad[slot][:, None]
        return jnp.concatenate([grad, spread[None]], axis=0).astype(bf16).reshape(5 * chans, total)

    keeps, sends, taps = [None] * 4, [None] * 4, [None] * 4
    for slot in (3, 2, 1, 0):
        grads = branch_grad(slot)
        keeps[slot], sends[slot], taps[slot] = weight_grads(
            grads, pixels, sel[None], columns, half
        )

    def add(*values):
        return sum(value.astype(f32) for value in values).astype(bf16)

    def z_sums(parts):
        first, near, second, third = parts
        mid_two = add(third, lax.ppermute(third, "z", INWARD))
        mid_one = add(second, lax.ppermute(second, "z", INWARD))
        near = add(near, lax.ppermute(mid_two, "z", MID))
        return add(first, lax.ppermute(near, "z", PAIR), lax.ppermute(mid_one, "z", MID))

    if halves:
        mixed = [None] * 4
        for slot in (3, 2, 1, 0):
            mixed[slot] = add(keeps[slot], lax.ppermute(sends[slot], "dp", SWAP))
        mine = z_sums(mixed)
        other = lax.ppermute(mine, "dp", SWAP)
        low_sum = jnp.where(x_id == 0, mine, other)
        high_sum = jnp.where(x_id == 0, other, mine)
    else:
        low_sum = lax.psum(z_sums(keeps), "dp")
        high_sum = lax.psum(z_sums(sends), "dp")
    branch_grads = jnp.concatenate(
        [
            low_sum.astype(f32).reshape(split + 1, chans, depth),
            high_sum.astype(f32).reshape(split + 1, chans, depth)[1:],
        ],
        axis=0,
    )

    flat_w = [part for slot in slots for part in slot]
    input_sel = jnp.stack(sels)
    cross = input_grads(
        taps, flat_w, input_sel, jnp.stack([quad_id ^ 3, quad_id ^ 1]), strip
    )
    cross = lax.ppermute(cross, "c", SWAP)
    own = input_grads(taps, flat_w, input_sel, jnp.stack([quad_id ^ 2, quad_id]), strip)
    far = add(own[0], cross[0])
    far = lax.ppermute(far, "y", SWAP)
    input_grad = (
        (own[1].astype(f32) + cross[1].astype(f32) + far.astype(f32)) * own_inside[:, None]
    ).astype(bf16)
    input_grad = input_grad.reshape(1, strip_rows, columns, depth)

    head_wgrad = lax.dot_general(
        unit_back, concat, (((1,), (1,)), ((), ())), preferred_element_type=f32
    )
    head_wgrad = head_wgrad.reshape(all_ch, 4, 16 * chans + 16)[:, :, : 16 * chans]
    head_wgrad = head_wgrad.reshape(all_ch, 4, 4, 4, chans)
    pool_wgrad = (row_sums[:, None] * all_pool[None]).reshape(all_ch, 4, 4, 1, chans)
    head_wgrad = jnp.concatenate([head_wgrad, pool_wgrad], axis=3).astype(bf16)
    spot = jnp.sum(place * jnp.arange(4, dtype=f32)[None], axis=1).astype(jnp.int32)
    head_wgrad = jnp.stack(
        [lax.dynamic_index_in_dim(head_wgrad, spot[at], 2, keepdims=False) for at in range(4)],
        axis=0,
    )
    head_wgrad = jnp.transpose(head_wgrad, (1, 3, 0, 2, 4)).reshape(all_ch, 5 * all_ch)
    head_grads = lax.psum_scatter(head_wgrad, PLANE, scatter_dimension=0, tiled=True)
    head_grads = lax.psum(head_grads.astype(f32), "dp")

    own_sums = lax.dynamic_index_in_dim(moments, z_id, 0, keepdims=False)
    own_head = lax.dynamic_slice_in_dim(head_moments, wide_id * chans, chans, 1)
    norm_grads = jnp.stack(
        [
            jnp.concatenate([own_sums[1], own_head[1][None]]),
            jnp.concatenate([own_sums[0], own_head[0][None]]),
        ]
    )
    own_centres = lax.dynamic_index_in_dim(centres, z_id, 0, keepdims=False)
    own_variances = lax.dynamic_index_in_dim(variances, z_id, 0, keepdims=False)
    head_stats = lax.dynamic_slice_in_dim(
        jnp.stack([head_centre, head_variance]), wide_id * chans, chans, 1
    )
    all_centres = jnp.concatenate([own_centres, head_stats[0][None]])
    all_variances = jnp.concatenate([own_variances, head_stats[1][None]])
    factors = jnp.where(
        jnp.arange(6) == 4, image_total / (image_total - 1.0), pixel_total / (pixel_total - 1.0)
    )
    running_next = (1.0 - momentum) * running_stats + momentum * jnp.stack(
        [all_centres, all_variances * factors[:, None]]
    )
    branch_means, branch_squares, branch_updated = adamw_update(
        branch_weight, branch_grads, branch_first, branch_second, conv_rate, weight_decay
    )
    head_means, head_squares, head_updated = adamw_update(
        head_weight, head_grads, head_first, head_second, conv_rate, weight_decay
    )
    norm_means, norm_squares, norm_updated = adamw_update(
        norm_params, norm_grads, norm_first, norm_second, norm_rate, 0.0
    )
    return (
        head_output,
        input_grad,
        branch_grads,
        branch_means,
        branch_squares,
        branch_updated,
        head_grads,
        head_means,
        head_squares,
        head_updated,
        norm_grads,
        norm_means,
        norm_squares,
        norm_updated,
        running_next,
    )


def solution(mesh):
    groups, wide = mesh.devices.shape
    fine = Mesh(mesh.devices.reshape(groups, 4, 2, wide // 8), ("dp",) + PLANE)
    placed = (
        P("dp", PLANE, None, None),
        P("dp", None),
        P("dp", PLANE, None),
        P(None, PLANE, None),
        P(None, PLANE, None),
        P(None, PLANE, None),
        P(PLANE, None),
        P(PLANE, None),
        P(PLANE, None),
        P(None, None, PLANE),
        P(None, None, PLANE),
        P(None, None, PLANE),
        P(None, None, PLANE),
    )
    return jax.shard_map(
        local,
        mesh=fine,
        in_specs=placed,
        out_specs=(
            P("dp", PLANE, None),
            P("dp", PLANE, None, None),
            P(None, PLANE, None),
            P(None, PLANE, None),
            P(None, PLANE, None),
            P(None, PLANE, None),
            P(PLANE, None),
            P(PLANE, None),
            P(PLANE, None),
            P(PLANE, None),
            P(None, None, PLANE),
            P(None, None, PLANE),
            P(None, None, PLANE),
            P(None, None, PLANE),
            P(None, None, PLANE),
        ),
        check_vma=False,
    )
```

time: 1590 us -> 588 us (0.37)
  waiting for transfers between devices: 1080 us -> 167 us
  matrix products: 168 us -> 6.02 us
  local copies, waits for them, and re-layouts: 203 us -> 51.7 us
  Pallas kernels: 0 us -> 99.4 us
  starting transfers between devices: 0.21 us -> 77.5 us
  blocking collectives: 29.9 us -> 73.8 us
    reduce_scatter x2 -> x1, waiting for transfers between devices: 710 us -> 0.01 us  [local(): lax.psum_scatter(head_wgrad, PLANE, scatter_dimension=0, tiled=True)]
    all_gather x2 -> x0, waiting for transfers between devices: 369 us -> none  [the longest x1 203 us: local(): full_concat = lax.all_gather(concat, 'wide', axis=4, tiled=True)]
    dot_general x6 -> x3, matrix products: 168 us -> 6.02 us  [the longest x1 2.78 us: local(): unit = jnp.dot(pixel_proj, concat, preferred_element_type=f32)]
    ppermute x0 -> x23, waiting for transfers between devices: none -> 138 us  [the longest x1 21.8 us: local(): far = lax.ppermute(far, 'y', SWAP)]
    pallas_call x0 -> x10, Pallas kernels: none -> 99.4 us  [the longest x4 35.3 us: forward_taps(): pl.pallas_call(functools.partial(forward_kernel, columns, split), out_sha...]
    slice x4 -> x26, local copies, waits for them, and re-layouts: 93.9 us -> 4.73 us  [the longest x2 2.87 us: local(): head_wgrad.reshape(all_ch, 4, 16 * chans + 16)[:, :, :16 * chans]]
    convert_element_type x3 -> x10, local copies, waits for them, and re-layouts: 77.9 us -> 8.4 us  [the longest x8 8.31 us: branch_delta(): return gelu_back(branch_norm(slot), concat_back[slot].astype(f32))]
    all_gather x0 -> x2, blocking collectives: none -> 64.8 us  [the longest x1 32.7 us: local(): lax.all_gather(norm_params, PLANE, axis=0).reshape(4, 4, 2, 6, chans)]
  transfers between devices with their start and end apart: 5 -> 32, of which waited for: 4 -> 15; matrix products, arithmetic and copies ran while one was open for 5% -> 13% of each run, Pallas kernels for 0% -> 16%
where the time goes in v1:
time: 588 us; the launch traced here: 583 us
  waiting for transfers between devices  167 us (28%)
  Pallas kernels  99.4 us (17%)
  starting transfers between devices  77.5 us (13%)
  other arithmetic  75.3 us (13%)
  blocking collectives  73.8 us (13%)
  local copies, waits for them, and re-layouts  51.7 us (9%)
  between operations  32.5 us (6%)
  matrix products  6.02 us (1%)
    pallas_call x4, Pallas kernels, forward_taps(): pl.pallas_call(functools.partial(forward_kernel, columns, split), out_sha...  35.3 us
    pallas_call x4, Pallas kernels, weight_grads(): pl.pallas_call(functools.partial(weight_kernel, columns), out_shape=(jax....  33.1 us
    all_gather x1, blocking collectives, local(): lax.all_gather(norm_params, PLANE, axis=0).reshape(4, 4, 2, 6, chans)  32.7 us
    all_gather x1, blocking collectives, local(): lax.all_gather(head_weight.astype(bf16), PLANE, axis=0, tiled=True)  32.1 us
    pallas_call x2, Pallas kernels, input_grads(): pl.pallas_call(functools.partial(input_kernel, start), out_shape=jax.Shap...  31 us
    all_to_all x4, starting transfers between devices, total_over(): return jnp.sum(lax.all_to_all(spread, axes, 0, 0, tiled=True), axis=0)  24 us
    ppermute x1, waiting for transfers between devices, local(): far = lax.ppermute(far, 'y', SWAP)  21.8 us
    ppermute x1, waiting for transfers between devices, z_chain(): near = lax.ppermute(block, 'z', PAIR)  21.3 us
  transfers between devices with their start and end apart: 32, of which 15 were waited for; matrix products, arithmetic and copies ran while one was open for 13% of the time, Pallas kernels for 16%

profile of v1, /device:TPU:0, one launch (start us, length us, event | category | flops | bytes accessed | tf_op | source)
XLA Modules:
  0.0 583.1 jit_solution(2327936248462546241)
XLA Ops:
  22.7 21.3 %collective-permute-done.3.wz_ref.refs_6_ = bf16[240,2048]{1,0:T(8,128)(2,1)} collective-permute-done((bf16[240,2048]{1,0:T(8,128)(2,1)}, bf16[240,2048]{1,0:T(8,128)(2,1)}, u32[]{:S(2)}, u32[]{:S(2)}) %collective-permute-start.3) | collective-permute-done | bytes 983072 | tf_op jit(solution)/shard_map/ppermute | solution.py:351
  45.6 32.7 %all-gather = f32[32,6,16]{2,1,0:T(8,128)S(1)} all-gather(f32[2,6,16]{2,1,0:T(8,128)S(1)} %copy.360), channel_id=2, replica_groups=mesh['dp'=2,'z'=4,'y'=2,'c'=2] {'z','y','c'}, dimensions={0}, use_global_device_ids=true | all-gather | bytes 13056 | tf_op jit(solution)/shard_map/all_gather | solution.py:390
  88.0 18.9 %collective-permute-done.8 = bf16[240,2048]{1,0:T(8,128)(2,1)} collective-permute-done((bf16[240,2048]{1,0:T(8,128)(2,1)S(1)}, bf16[240,2048]{1,0:T(8,128)(2,1)}, u32[]{:S(2)}, u32[]{:S(2)}) %collective-permute-start.8) | collective-permute-done | bytes 983072 | tf_op jit(solution)/shard_map/ppermute | solution.py:354
  108.3 19.2 %collective-permute-done.6 = bf16[240,2048]{1,0:T(8,128)(2,1)} collective-permute-done((bf16[240,2048]{1,0:T(8,128)(2,1)}, bf16[240,2048]{1,0:T(8,128)(2,1)}, u32[]{:S(2)}, u32[]{:S(2)}) %collective-permute-start.6) | collective-permute-done | bytes 983072 | tf_op jit(solution)/shard_map/ppermute | solution.py:355
  141.2 8.8 %atrous_forward.4 = (f32[4,16,2048]{2,1,0:T(8,128)}, f32[64,128]{1,0:T(8,128)}) custom-call(s32[1]{0:T(128)} %constant.185.clone.1.sel_ref, bf16[2048,2048]{1,0:T(8,128)(2,1)} %constant_dynamic-update-slice_fusion.x_ref, bf16[240,2048]{1,0:T(8,128)(2,1)} %bitcast.265, bf16[240,2048]{1,0:T(8,128)(2,1)} %bitcast.268, f32[8,2048]{1,0:T(8,128)} %broadcast_in_dim.27.mask_ref), custom_call_target="tpu_custom_call" | custom-call | flops 4026531840 | bytes 10878976 | tf_op jit(solution)/shard_map/atrous_forward/pallas_call | solution.py:144
  154.5 8.8 %atrous_forward.7 = (f32[4,16,2048]{2,1,0:T(8,128)}, f32[64,128]{1,0:T(8,128)}) custom-call(s32[1]{0:T(128)} %bitcast.22.sel_ref, bf16[2048,2048]{1,0:T(8,128)(2,1)} %constant_dynamic-update-slice_fusion.x_ref, bf16[240,2048]{1,0:T(8,128)(2,1)} %copy-done.25, bf16[240,2048]{1,0:T(8,128)(2,1)} %copy-done.105, f32[8,2048]{1,0:T(8,128)} %broadcast_in_dim.27.mask_ref), custom_call_target="tpu_custom_call" | custom-call | flops 4026531840 | bytes 10878976 | tf_op jit(solution)/shard_map/atrous_forward/pallas_call | solution.py:144
  163.4 9.8 %collective-permute-done.9.wx_ref.refs_9_ = bf16[240,2048]{1,0:T(8,128)(2,1)S(1)} collective-permute-done((bf16[240,2048]{1,0:T(8,128)(2,1)S(1)}, bf16[240,2048]{1,0:T(8,128)(2,1)S(1)}, u32[]{:S(2)}, u32[]{:S(2)}) %collective-permute-start.9) | collective-permute-done | bytes 983072 | tf_op jit(solution)/shard_map/ppermute | solution.py:363
  174.2 8.8 %atrous_forward.6 = (f32[4,16,2048]{2,1,0:T(8,128)}, f32[64,128]{1,0:T(8,128)}) custom-call(s32[1]{0:T(128)} %bitcast.22.sel_ref, bf16[2048,2048]{1,0:T(8,128)(2,1)} %constant_dynamic-update-slice_fusion.x_ref, bf16[240,2048]{1,0:T(8,128)(2,1)} %copy-done.24, bf16[240,2048]{1,0:T(8,128)(2,1)} %copy-done.106, f32[8,2048]{1,0:T(8,128)} %broadcast_in_dim.27.mask_ref), custom_call_target="tpu_custom_call" | custom-call | flops 4026531840 | bytes 10878976 | tf_op jit(solution)/shard_map/atrous_forward/pallas_call | solution.py:144
  184.0 8.8 %atrous_forward.5 = (f32[4,16,2048]{2,1,0:T(8,128)}, f32[64,128]{1,0:T(8,128)}) custom-call(s32[1]{0:T(128)} %bitcast.22.sel_ref, bf16[2048,2048]{1,0:T(8,128)(2,1)} %constant_dynamic-update-slice_fusion.x_ref, bf16[240,2048]{1,0:T(8,128)(2,1)} %collective-permute-done.3.wz_ref.refs_6_, bf16[240,2048]{1,0:T(8,128)(2,1)} %copy-done.104, ...), custom_call_target="tpu_custom_call" | custom-call | flops 4026531840 | bytes 10878976 | tf_op jit(solution)/shard_map/atrous_forward/pallas_call | solution.py:144
  196.0 15.5 %all-to-all-start = ((f32[8,1,704]{2,1,0:T(1,128)}), f32[8,1,704]{2,1,0:T(1,128)S(1)}, u32[]{:S(2)}, u32[]{:S(2)}) async-start(f32[8,1,704]{2,1,0:T(1,128)} %reshape.882), calls=%async_computation | async-start | bytes 49152 | tf_op jit(solution)/shard_map/all_to_all | solution.py:58
  238.8 32.1 %all_gather.11 = bf16[256,1280]{1,0:T(8,128)(2,1)S(1)} all-gather(bf16[16,1280]{1,0:T(8,128)(2,1)S(1)} %convert_element_type.300), channel_id=1, replica_groups=mesh['dp'=2,'z'=4,'y'=2,'c'=2] {'z','y','c'}, dimensions={0}, use_global_device_ids=true | all-gather | bytes 696320 | tf_op jit(solution)/shard_map/all_gather | solution.py:395
  298.7 8.7 %all-to-all-done.4 = bf16[16,16,512]{2,0,1:T(8,128)(2,1)} async-done(((bf16[16,16,512]{2,0,1:T(8,128)(2,1)}), bf16[16,16,512]{2,0,1:T(8,128)(2,1)}, u32[]{:S(2)}, u32[]{:S(2)}) %all-to-all-start.4) | async-done | bytes 262176 | tf_op jit(solution)/shard_map/all_to_all | solution.py:406
  338.6 7.0 %all-to-all-done.6 = bf16[4,272,512]{2,1,0:T(8,128)(2,1)S(1)} async-done(((bf16[4,272,512]{2,1,0:T(8,128)(2,1)}), bf16[4,272,512]{2,1,0:T(8,128)(2,1)S(1)}, u32[]{:S(2)}, u32[]{:S(2)}) %all-to-all-start.6) | async-done | bytes 1114144 | tf_op jit(solution)/shard_map/all_to_all | solution.py:510
  383.6 8.2 %atrous_weight_grad.5 = (bf16[240,2048]{1,0:T(8,128)(2,1)}, bf16[240,2048]{1,0:T(8,128)(2,1)}, bf16[464,2048]{1,0:T(8,128)(2,1)}) custom-call(s32[1]{0:T(128)} %bitcast.22.sel_ref, bf16[80,2048]{1,0:T(8,128)(2,1)} %bitcast.283, bf16[2048,2048]{1,0:T(8,128)(2,1)} %constant_dynamic-update-slice_fusion.x_ref), custom_call_target="tpu_custom_call" | custom-call | flops 3892314112 | bytes 12320768 | tf_op jit(solution)/shard_map/atrous_weight_grad/pallas_call | solution.py:219
  393.3 8.3 %atrous_weight_grad.7 = (bf16[240,2048]{1,0:T(8,128)(2,1)}, bf16[240,2048]{1,0:T(8,128)(2,1)}, bf16[464,2048]{1,0:T(8,128)(2,1)}) custom-call(s32[1]{0:T(128)} %bitcast.22.sel_ref, bf16[80,2048]{1,0:T(8,128)(2,1)} %bitcast.284, bf16[2048,2048]{1,0:T(8,128)(2,1)} %constant_dynamic-update-slice_fusion.x_ref), custom_call_target="tpu_custom_call" | custom-call | flops 3892314112 | bytes 12320768 | tf_op jit(solution)/shard_map/atrous_weight_grad/pallas_call | solution.py:219
  405.4 8.2 %atrous_weight_grad.6 = (bf16[240,2048]{1,0:T(8,128)(2,1)}, bf16[240,2048]{1,0:T(8,128)(2,1)}, bf16[464,2048]{1,0:T(8,128)(2,1)}) custom-call(s32[1]{0:T(128)} %bitcast.22.sel_ref, bf16[80,2048]{1,0:T(8,128)(2,1)} %bitcast.285, bf16[2048,2048]{1,0:T(8,128)(2,1)} %constant_dynamic-update-slice_fusion.x_ref), custom_call_target="tpu_custom_call" | custom-call | flops 3892314112 | bytes 12320768 | tf_op jit(solution)/shard_map/atrous_weight_grad/pallas_call | solution.py:219
  415.0 8.3 %atrous_weight_grad.4 = (bf16[240,2048]{1,0:T(8,128)(2,1)}, bf16[240,2048]{1,0:T(8,128)(2,1)}, bf16[464,2048]{1,0:T(8,128)(2,1)}) custom-call(s32[1]{0:T(128)} %bitcast.22.sel_ref, bf16[80,2048]{1,0:T(8,128)(2,1)} %bitcast.282, bf16[2048,2048]{1,0:T(8,128)(2,1)} %constant_dynamic-update-slice_fusion.x_ref), custom_call_target="tpu_custom_call" | custom-call | flops 3892314112 | bytes 12320768 | tf_op jit(solution)/shard_map/atrous_weight_grad/pallas_call | solution.py:219
  423.3 14.4 %collective-permute-done.15 = bf16[240,2048]{1,0:T(8,128)(2,1)S(1)} collective-permute-done((bf16[240,2048]{1,0:T(8,128)(2,1)}, bf16[240,2048]{1,0:T(8,128)(2,1)S(1)}, u32[]{:S(2)}, u32[]{:S(2)}) %collective-permute-start.15) | collective-permute-done | bytes 983072 | tf_op jit(solution)/shard_map/ppermute | solution.py:577
  442.0 15.5 %atrous_input_grad.3 = bf16[2,512,2048]{2,1,0:T(8,128)(2,1)} custom-call(s32[4]{0:T(128)} %pad_add_fusion.1.sel_ref, s32[2]{0:T(128)} %pad_add_fusion.3.strip_ref, bf16[464,2048]{1,0:T(8,128)(2,1)} %get-tuple-element.47.refs_0_, bf16[464,2048]{1,0:T(8,128)(2,1)} %get-tuple-element.48.refs_1_, bf16[464,2048]{1,0:T(8,128)(2,1)} %get-tuple-element.49.refs_2_, ...), custom_call_target="tpu_custom_call" | custom-call | flops 7784628224 | bytes 12058624 | tf_op jit(solution)/shard_map/atrous_input_grad/pallas_call | solution.py:278
  468.3 14.5 %collective-permute-done.20 = bf16[240,2048]{1,0:T(8,128)(2,1)} collective-permute-done((bf16[240,2048]{1,0:T(8,128)(2,1)S(1)}, bf16[240,2048]{1,0:T(8,128)(2,1)}, u32[]{:S(2)}, u32[]{:S(2)}) %collective-permute-start.20) | collective-permute-done | bytes 983072 | tf_op jit(solution)/shard_map/ppermute | solution.py:570
  495.1 15.5 %atrous_input_grad.2 = bf16[2,512,2048]{2,1,0:T(8,128)(2,1)} custom-call(s32[4]{0:T(128)} %pad_add_fusion.1.sel_ref, s32[2]{0:T(128)} %pad_add_fusion.2.strip_ref, bf16[464,2048]{1,0:T(8,128)(2,1)} %get-tuple-element.47.refs_0_, bf16[464,2048]{1,0:T(8,128)(2,1)} %get-tuple-element.48.refs_1_, bf16[464,2048]{1,0:T(8,128)(2,1)} %get-tuple-element.49.refs_2_, ...), custom_call_target="tpu_custom_call" | custom-call | flops 7784628224 | bytes 12058624 | tf_op jit(solution)/shard_map/atrous_input_grad/pallas_call | solution.py:278
  510.6 9.0 %all-reduce.6 = f32[16,1280]{1,0:T(8,128)S(1)} all-reduce(bf16[16,1280]{1,0:T(8,128)(2,1)} %reduce-scatter.4.cloned.1.call-done), channel_id=1, replica_groups=mesh['dp'=2,'z'=4,'y'=2,'c'=2] {'dp'}, use_global_device_ids=true, to_apply=%region_28.29 | all-reduce | flops 20480 | bytes 122880 | tf_op jit(solution)/shard_map/psum | solution.py:621
  529.1 13.8 %collective-permute-done.22 = bf16[240,2048]{1,0:T(8,128)(2,1)S(1)} collective-permute-done((bf16[240,2048]{1,0:T(8,128)(2,1)S(1)}, bf16[240,2048]{1,0:T(8,128)(2,1)S(1)}, u32[]{:S(2)}, u32[]{:S(2)}) %collective-permute-start.22) | collective-permute-done | bytes 983072 | tf_op jit(solution)/shard_map/ppermute | solution.py:579
  549.8 21.8 %collective-permute-done.12 = bf16[512,2048]{1,0:T(8,128)(2,1)S(1)} collective-permute-done((bf16[512,2048]{1,0:T(8,128)(2,1)S(1)}, bf16[512,2048]{1,0:T(8,128)(2,1)S(1)}, u32[]{:S(2)}, u32[]{:S(2)}) %collective-permute-start.12) | collective-permute-done | bytes 2097184 | tf_op jit(solution)/shard_map/ppermute | solution.py:601
  (477 shorter events, 212.4 us)
Async XLA Ops:
  13.8 71.3 %collective-permute-start.1 = (bf16[512,2048]{1,0:T(8,128)(2,1)}, bf16[512,2048]{1,0:T(8,128)(2,1)}, u32[]{:S(2)}, u32[]{:S(2)}) collective-permute-start(bf16[512,2048]{1,0:T(8,128)(2,1)} %get-tuple-element.305), channel_id=1, source_target_pairs={{0,2},{2,0},{1,3},{3,1},{4,6},{6,4},{5,7},{7,5},{8,10},{10,8},{9,1... | collective-permute-start | bytes 6291464 | tf_op jit(solution)/shard_map/ppermute | solution.py:347
  18.9 25.1 %collective-permute-start.3 = (bf16[240,2048]{1,0:T(8,128)(2,1)}, bf16[240,2048]{1,0:T(8,128)(2,1)}, u32[]{:S(2)}, u32[]{:S(2)}) collective-permute-start(bf16[240,2048]{1,0:T(8,128)(2,1)} %broadcast_select_fusion.3), channel_id=1, source_target_pairs={{0,4},{4,0},{8,12},{12,8},{1,5},{5,1},{9,13},{13,9},{2,6},{6,2},{1... | collective-permute-start | bytes 2949128 | tf_op jit(solution)/shard_map/ppermute | solution.py:351
  22.0 58.4 %collective-permute-start.7 = (bf16[240,2048]{1,0:T(8,128)(2,1)}, bf16[240,2048]{1,0:T(8,128)(2,1)S(1)}, u32[]{:S(2)}, u32[]{:S(2)}) collective-permute-start(bf16[240,2048]{1,0:T(8,128)(2,1)} %broadcast_select_fusion.3), channel_id=1, source_target_pairs={{4,8},{8,4},{5,9},{9,5},{6,10},{10,6},{7,11},{11,7},{20,24},{24,20... | collective-permute-start | bytes 2949128 | tf_op jit(solution)/shard_map/ppermute | solution.py:352
  44.0 39.8 %collective-permute-start.5 = (bf16[240,2048]{1,0:T(8,128)(2,1)}, bf16[240,2048]{1,0:T(8,128)(2,1)}, u32[]{:S(2)}, u32[]{:S(2)}) collective-permute-start(bf16[240,2048]{1,0:T(8,128)(2,1)} %collective-permute-done.3.wz_ref.refs_6_), channel_id=1, source_target_pairs={{4,8},{8,4},{5,9},{9,5},{6,10},{10,6},{7,11},{11,7},{20,24},{24,20... | collective-permute-start | bytes 2949128 | tf_op jit(solution)/shard_map/ppermute | solution.py:353
  45.6 84.7 %collective-permute-start = (bf16[512,2048]{1,0:T(8,128)(2,1)}, bf16[512,2048]{1,0:T(8,128)(2,1)}, u32[]{:S(2)}, u32[]{:S(2)}) collective-permute-start(bf16[512,2048]{1,0:T(8,128)(2,1)} %get-tuple-element.305), channel_id=1, source_target_pairs={{0,1},{1,0},{2,3},{3,2},{4,5},{5,4},{6,7},{7,6},{8,9},{9,8},{10,11... | collective-permute-start | bytes 6291464 | tf_op jit(solution)/shard_map/ppermute | solution.py:346
  80.4 26.6 %collective-permute-start.8 = (bf16[240,2048]{1,0:T(8,128)(2,1)S(1)}, bf16[240,2048]{1,0:T(8,128)(2,1)}, u32[]{:S(2)}, u32[]{:S(2)}) collective-permute-start(bf16[240,2048]{1,0:T(8,128)(2,1)S(1)} %collective-permute-done.7), channel_id=1, source_target_pairs={{4,0},{8,12},{5,1},{9,13},{6,2},{10,14},{7,3},{11,15},{20,16},{24,... | collective-permute-start | bytes 2949128 | tf_op jit(solution)/shard_map/ppermute | solution.py:354
  83.8 43.7 %collective-permute-start.6 = (bf16[240,2048]{1,0:T(8,128)(2,1)}, bf16[240,2048]{1,0:T(8,128)(2,1)}, u32[]{:S(2)}, u32[]{:S(2)}) collective-permute-start(bf16[240,2048]{1,0:T(8,128)(2,1)} %collective-permute-done.5), channel_id=1, source_target_pairs={{4,0},{8,12},{5,1},{9,13},{6,2},{10,14},{7,3},{11,15},{20,16},{24,... | collective-permute-start | bytes 2949128 | tf_op jit(solution)/shard_map/ppermute | solution.py:355
  85.1 52.2 %collective-permute-start.2 = (bf16[512,2048]{1,0:T(8,128)(2,1)}, bf16[512,2048]{1,0:T(8,128)(2,1)}, u32[]{:S(2)}, u32[]{:S(2)}) collective-permute-start(bf16[512,2048]{1,0:T(8,128)(2,1)} %collective-permute-done.1), channel_id=1, source_target_pairs={{0,1},{1,0},{2,3},{3,2},{4,5},{5,4},{6,7},{7,6},{8,9},{9,8},{10,11... | collective-permute-start | bytes 6291464 | tf_op jit(solution)/shard_map/ppermute | solution.py:348
  86.5 96.5 %collective-permute-start.4 = (bf16[240,2048]{1,0:T(8,128)(2,1)}, bf16[240,2048]{1,0:T(8,128)(2,1)S(1)}, u32[]{:S(2)}, u32[]{:S(2)}) collective-permute-start(bf16[240,2048]{1,0:T(8,128)(2,1)} %collective-permute-done.3.wz_ref.refs_6_), channel_id=1, source_target_pairs={{0,16},{16,0},{1,17},{17,1},{2,18},{18,2},{3,19},{19,3},{4,20},{20... | collective-permute-start | bytes 2949128 | tf_op jit(solution)/shard_map/ppermute | solution.py:363
  128.8 24.7 %collective-permute-start.10 = (bf16[240,2048]{1,0:T(8,128)(2,1)S(1)}, bf16[240,2048]{1,0:T(8,128)(2,1)S(1)}, u32[]{:S(2)}, u32[]{:S(2)}) collective-permute-start(bf16[240,2048]{1,0:T(8,128)(2,1)S(1)} %broadcast_select_fusion.wz_ref.refs_10_), channel_id=1, source_target_pairs={{0,16},{16,0},{1,17},{17,1},{2,18},{18,2},{3,19},{19,3},{4,20},{20... | collective-permute-start | bytes 2949128 | tf_op jit(solution)/shard_map/ppermute | solution.py:363
  136.8 36.4 %collective-permute-start.9 = (bf16[240,2048]{1,0:T(8,128)(2,1)S(1)}, bf16[240,2048]{1,0:T(8,128)(2,1)S(1)}, u32[]{:S(2)}, u32[]{:S(2)}) collective-permute-start(bf16[240,2048]{1,0:T(8,128)(2,1)S(1)} %broadcast_select_fusion.1.wz_ref.refs_8_), channel_id=1, source_target_pairs={{0,16},{16,0},{1,17},{17,1},{2,18},{18,2},{3,19},{19,3},{4,20},{20... | collective-permute-start | bytes 2949128 | tf_op jit(solution)/shard_map/ppermute | solution.py:363
  196.0 27.9 %all-to-all-start = ((f32[8,1,704]{2,1,0:T(1,128)}), f32[8,1,704]{2,1,0:T(1,128)S(1)}, u32[]{:S(2)}, u32[]{:S(2)}) async-start(f32[8,1,704]{2,1,0:T(1,128)} %reshape.882), calls=%async_computation | async-start | bytes 49152 | tf_op jit(solution)/shard_map/all_to_all | solution.py:58
  234.5 44.2 %all-to-all-start.1 = ((bf16[4,272,512]{2,1,0:T(8,128)(2,1)}), bf16[4,272,512]{2,1,0:T(8,128)(2,1)}, u32[]{:S(2)}, u32[]{:S(2)}) async-start(bf16[4,272,512]{2,1,0:T(8,128)(2,1)} %pad_maximum_fusion), calls=%async_computation.1 | async-start | bytes 2228224 | tf_op jit(solution)/shard_map/all_to_all | solution.py:461
  365.9 144.7 %reduce-scatter.4.cloned.1.call-start = ((), (), s32[]{:S(2)}) async-start(), calls=%async_computation.9 | async-start | bytes 696320 | tf_op jit(solution)/shard_map/reduce_scatter | solution.py:620
  372.5 94.1 %all-to-all-start.3 = ((bf16[16,16,512]{2,1,0:T(8,128)(2,1)}), bf16[16,16,512]{2,1,0:T(8,128)(2,1)S(1)}, u32[]{:S(2)}, u32[]{:S(2)}) async-start(bf16[16,16,512]{2,1,0:T(8,128)(2,1)} %bitcast.281), calls=%async_computation.3 | async-start | bytes 524288 | tf_op jit(solution)/shard_map/all_to_all | solution.py:481
  391.9 94.2 %collective-permute-start.14 = (bf16[240,2048]{1,0:T(8,128)(2,1)}, bf16[240,2048]{1,0:T(8,128)(2,1)}, u32[]{:S(2)}, u32[]{:S(2)}) collective-permute-start(bf16[240,2048]{1,0:T(8,128)(2,1)} %get-tuple-element.54), channel_id=1, source_target_pairs={{0,16},{16,0},{1,17},{17,1},{2,18},{18,2},{3,19},{19,3},{4,20},{20... | collective-permute-start | bytes 2949128 | tf_op jit(solution)/shard_map/ppermute | solution.py:577
  401.6 36.2 %collective-permute-start.15 = (bf16[240,2048]{1,0:T(8,128)(2,1)}, bf16[240,2048]{1,0:T(8,128)(2,1)S(1)}, u32[]{:S(2)}, u32[]{:S(2)}) collective-permute-start(bf16[240,2048]{1,0:T(8,128)(2,1)} %get-tuple-element.56), channel_id=1, source_target_pairs={{0,16},{16,0},{1,17},{17,1},{2,18},{18,2},{3,19},{19,3},{4,20},{20... | collective-permute-start | bytes 2949128 | tf_op jit(solution)/shard_map/ppermute | solution.py:577
  413.7 44.6 %collective-permute-start.19 = (bf16[240,2048]{1,0:T(8,128)(2,1)}, bf16[240,2048]{1,0:T(8,128)(2,1)S(1)}, u32[]{:S(2)}, u32[]{:S(2)}) collective-permute-start(bf16[240,2048]{1,0:T(8,128)(2,1)} %get-tuple-element.58), channel_id=1, source_target_pairs={{0,16},{16,0},{1,17},{17,1},{2,18},{18,2},{3,19},{19,3},{4,20},{20... | collective-permute-start | bytes 2949128 | tf_op jit(solution)/shard_map/ppermute | solution.py:577
  438.1 25.1 %collective-permute-start.16 = (bf16[240,2048]{1,0:T(8,128)(2,1)S(1)}, bf16[240,2048]{1,0:T(8,128)(2,1)S(1)}, u32[]{:S(2)}, u32[]{:S(2)}) collective-permute-start(bf16[240,2048]{1,0:T(8,128)(2,1)S(1)} %add_convert_fusion.6), channel_id=1, source_target_pairs={{0,4},{12,8},{1,5},{13,9},{2,6},{14,10},{3,7},{15,11},{16,20},{28,... | collective-permute-start | bytes 2949128 | tf_op jit(solution)/shard_map/ppermute | solution.py:569
  457.5 67.3 %collective-permute-start.11 = (bf16[2,512,2048]{2,1,0:T(8,128)(2,1)}, bf16[2,512,2048]{2,1,0:T(8,128)(2,1)}, u32[]{:S(2)}, u32[]{:S(2)}) collective-permute-start(bf16[2,512,2048]{2,1,0:T(8,128)(2,1)} %atrous_input_grad.3), channel_id=1, source_target_pairs={{0,1},{1,0},{2,3},{3,2},{4,5},{5,4},{6,7},{7,6},{8,9},{9,8},{10,11... | collective-permute-start | bytes 12582920 | tf_op jit(solution)/shard_map/ppermute | solution.py:598
  467.7 51.9 %collective-permute-start.13 = (bf16[240,2048]{1,0:T(8,128)(2,1)}, bf16[240,2048]{1,0:T(8,128)(2,1)S(1)}, u32[]{:S(2)}, u32[]{:S(2)}) collective-permute-start(bf16[240,2048]{1,0:T(8,128)(2,1)} %get-tuple-element.52), channel_id=1, source_target_pairs={{0,16},{16,0},{1,17},{17,1},{2,18},{18,2},{3,19},{19,3},{4,20},{20... | collective-permute-start | bytes 2949128 | tf_op jit(solution)/shard_map/ppermute | solution.py:577
  485.3 34.3 %collective-permute-start.21 = (bf16[240,2048]{1,0:T(8,128)(2,1)}, bf16[240,2048]{1,0:T(8,128)(2,1)S(1)}, u32[]{:S(2)}, u32[]{:S(2)}) collective-permute-start(bf16[240,2048]{1,0:T(8,128)(2,1)} %add_convert_fusion.2), channel_id=1, source_target_pairs={{4,8},{8,4},{5,9},{9,5},{6,10},{10,6},{7,11},{11,7},{20,24},{24,20... | collective-permute-start | bytes 2949128 | tf_op jit(solution)/shard_map/ppermute | solution.py:572
  489.2 30.4 %collective-permute-start.18 = (bf16[240,2048]{1,0:T(8,128)(2,1)}, bf16[240,2048]{1,0:T(8,128)(2,1)}, u32[]{:S(2)}, u32[]{:S(2)}) collective-permute-start(bf16[240,2048]{1,0:T(8,128)(2,1)} %add_convert_fusion.4), channel_id=1, source_target_pairs={{0,4},{4,0},{8,12},{12,8},{1,5},{5,1},{9,13},{13,9},{2,6},{6,2},{1... | collective-permute-start | bytes 2949128 | tf_op jit(solution)/shard_map/ppermute | solution.py:572
  527.5 44.1 %collective-permute-start.12 = (bf16[512,2048]{1,0:T(8,128)(2,1)S(1)}, bf16[512,2048]{1,0:T(8,128)(2,1)S(1)}, u32[]{:S(2)}, u32[]{:S(2)}) collective-permute-start(bf16[512,2048]{1,0:T(8,128)(2,1)S(1)} %fusion.4), channel_id=1, source_target_pairs={{0,2},{2,0},{1,3},{3,1},{4,6},{6,4},{5,7},{7,5},{8,10},{10,8},{9,1... | collective-permute-start | bytes 6291464 | tf_op jit(solution)/shard_map/ppermute | solution.py:601
  (118 other events, 3222.8 us)
Sparse Core Ops, SparseCore 0:
  370.3 56.6 reduce-scatter.3
